TPU v7x, 128 devices: a whole 4x4x4 slice. The times are simulated.
128 devices in a mesh: blk: 16 (over z, x_lo, core), uly: 8 (over x_hi, y).
Axes of the slice: x: 4 (x_hi: 2, x_lo: 2; x = x_hi * 2 + x_lo), y: 4, z: 4, core: 2. Of those that a mesh axis runs over, the one named last changes fastest.
Arguments:
- queries: bfloat16 [18432, 5120], P(('blk', 'uly')), may hold values from -6 to 6
- keys: bfloat16 [36864, 5120], P(('blk', 'uly')), may hold values from -6 to 6
- values: bfloat16 [36864, 5120], P(('blk', 'uly')), may hold values from -6 to 6
- tile_lists: int32 [48, 12], replicated, may hold values from 0 to 95, as said below
- tile_counts: int32 [48], replicated, may hold values from 3 to 12, as said below
Outputs:
- attended: bfloat16 [18432, 5120], P(('blk', 'uly'))
Inputs may be any that keep to these rules, and one draw needn't show every extreme that they name: `tile_lists`: entries lie in tiles of the latent frames from two before to two after the query tile's frame (frames are 3 tiles, blocks two frames); entry 0 is the query tile itself; the first tile_counts entries are distinct; the others repeat entry 0. `tile_counts`: counts vary from tile to tile; at least 3.
All inputs are finite; a program needn't handle non-finite values.
Results may differ from a plain program's by a relative error of at most 0.017.
Values may be sent and summed in bfloat16 or wider, within the bound.
A program may use at most 192 MiB of HBM per device.

v0:
```python
import jax
import jax.numpy as jnp
from jax import lax
from jax.sharding import PartitionSpec as P

HD = 128
TILE = 384
FT = 3
MAXT = 12


def shifted(array, axis, by):
    length = lax.axis_size(axis)
    pairs = [(i, i + by) for i in range(length) if 0 <= i + by < length]
    return lax.ppermute(array, axis, pairs)


def score_tile(query_tile, key_rows, value_rows, usable):
    score_scale = HD ** (-0.5)
    scores = (
        jnp.einsum("qhd,khd->hqk", query_tile, key_rows, preferred_element_type=jnp.float32)
        * score_scale
    )
    scores = jnp.where(usable[None, None, :], scores, -1e30)
    peak = jnp.max(scores, axis=-1)
    weights = jnp.where(usable[None, None, :], jnp.exp(scores - peak[:, :, None]), 0.0)
    denominator = jnp.sum(weights, axis=-1)
    rounded = weights.astype(jnp.bfloat16)
    summed = jnp.einsum("hqk,khd->qhd", rounded, value_rows, preferred_element_type=jnp.float32)
    return (summed, peak, denominator)


def finish(summed, denominator):
    return (summed / jnp.transpose(denominator, (0, 2, 1))[:, :, :, None]).astype(jnp.bfloat16)


def partial_tiles(query_tiles, key_tiles, value_tiles, lists_here, counts_here, limit):
    slot_ids = jnp.arange(MAXT, dtype=jnp.int32)
    heads_local = key_tiles.shape[2]

    def one_tile(inputs):
        query_tile, listed, count_here = inputs
        inside = (listed >= 0) & (listed < limit)
        safe_ids = jnp.clip(listed, 0, limit - 1)
        key_rows = jnp.take(key_tiles, safe_ids, axis=0).reshape(MAXT * TILE, heads_local, HD)
        value_rows = jnp.take(value_tiles, safe_ids, axis=0).reshape(MAXT * TILE, heads_local, HD)
        usable = jnp.repeat((slot_ids < count_here) & inside, TILE)
        return score_tile(query_tile, key_rows, value_rows, usable)

    return lax.map(one_tile, (query_tiles, lists_here, counts_here))


def per_device(queries, keys, values, tile_lists, tile_counts):
    query_heads, key_heads, value_heads = (
        lax.all_to_all(queries, "uly", split_axis=1, concat_axis=0, tiled=True),
        lax.all_to_all(keys, "uly", split_axis=1, concat_axis=0, tiled=True),
        lax.all_to_all(values, "uly", split_axis=1, concat_axis=0, tiled=True),
    )
    block_rows = key_heads.shape[0]
    local_width = key_heads.shape[1]
    heads_local = local_width // HD
    tiles_block = block_rows // TILE
    shard_index = lax.axis_index("blk")
    own_lists = lax.dynamic_slice_in_dim(tile_lists, shard_index * FT, FT, 0)
    own_counts = lax.dynamic_slice_in_dim(tile_counts, shard_index * FT, FT, 0)
    query_tiles = query_heads.reshape(FT, TILE, heads_local, HD)
    key_before, value_before = shifted((key_heads, value_heads), "blk", 1)
    key_after, value_after = shifted((key_heads, value_heads), "blk", -1)
    key_rows_all = jnp.concatenate([key_before, key_heads, key_after], axis=0)
    value_rows_all = jnp.concatenate([value_before, value_heads, value_after], axis=0)
    local_lists = own_lists - (shard_index - 1) * tiles_block
    key_tiles = key_rows_all.reshape(-1, TILE, heads_local, HD)
    value_tiles = value_rows_all.reshape(-1, TILE, heads_local, HD)
    summed, peak, denominator = partial_tiles(
        query_tiles, key_tiles, value_tiles, local_lists, own_counts, key_tiles.shape[0]
    )
    attended = finish(summed, denominator)
    attended = attended.reshape(FT * TILE, local_width)
    return lax.all_to_all(attended, "uly", split_axis=0, concat_axis=1, tiled=True)


def solution(mesh):
    placed = (P(("blk", "uly"), None), P(("blk", "uly"), None), P(("blk", "uly"), None), P(), P())
    return jax.shard_map(
        per_device, mesh=mesh, in_specs=placed, out_specs=P(("blk", "uly"), None), check_vma=False
    )
```

profile of v0, /device:TPU:64, one launch (start us, length us, event | category | flops | bytes accessed | tf_op | source)
XLA Modules:
  0.0 657.3 jit_solution(10457912884261272654)
XLA Ops:
  14.3 31.8 %all-to-all-done.2 = bf16[288,8,640]{2,0,1:T(8,128)(2,1)S(1)} async-done(((bf16[288,8,640]{2,0,1:T(8,128)(2,1)}), bf16[288,8,640]{2,0,1:T(8,128)(2,1)S(1)}, u32[]{:S(2)}, u32[]{:S(2)}) %all-to-all-start.2) | async-done | bytes 2949152 | tf_op jit(solution)/shard_map/all_to_all | solution.py:56
  59.0 30.5 %all-to-all-done = bf16[288,8,640]{2,0,1:T(8,128)(2,1)S(1)} async-done(((bf16[288,8,640]{2,0,1:T(8,128)(2,1)}), bf16[288,8,640]{2,0,1:T(8,128)(2,1)S(1)}, u32[]{:S(2)}, u32[]{:S(2)}) %all-to-all-start) | async-done | bytes 2949152 | tf_op jit(solution)/shard_map/all_to_all | solution.py:57
  103.1 127.4 %all-to-all-done.1 = bf16[144,8,640]{2,0,1:T(8,128)(2,1)} async-done(((bf16[144,8,640]{2,0,1:T(8,128)(2,1)}), bf16[144,8,640]{2,0,1:T(8,128)(2,1)}, u32[]{:S(2)}, u32[]{:S(2)}) %all-to-all-start.1) | async-done | bytes 1474592 | tf_op jit(solution)/shard_map/all_to_all | solution.py:55
  246.7 20.0 %reshape.76 = bf16[18,384,5,128]{3,2,1,0:T(8,128)(2,1)} reshape(bf16[6912,640]{1,0:T(8,128)(2,1)} %pad_maximum_fusion.1) | data formatting | bytes 17694720 | tf_op jit(solution)/shard_map/reshape | solution.py:72
  274.3 20.2 %reshape.75 = bf16[18,384,5,128]{3,2,1,0:T(8,128)(2,1)} reshape(bf16[6912,640]{1,0:T(8,128)(2,1)} %pad_maximum_fusion) | data formatting | bytes 17694720 | tf_op jit(solution)/shard_map/reshape | solution.py:73
  294.5 329.2 %while.13 = (s32[]{:T(128)}, f32[3,384,5,128]{1,3,2,0:T(8,128)S(1)}, f32[3,5,384]{2,1,0:T(8,128)S(1)}, s32[3,12]{1,0:T(4,128)S(1)}, bf16[18,384,5,128]{3,2,1,0:T...) while((s32[]{:T(128)}, ...), condition=%wide.region_3.5_spmd.clone, body=%wide.region_0.4_spmd.clone.sunk | while | flops 4606531584 | bytes 170219920 | solution.py:50
  306.4 10.6 %gather_fusion.1 = bf16[12,384,5,128]{3,2,1,0:T(8,128)(2,1)} fusion(bf16[18,384,5,128]{3,2,1,0:T(8,128)(2,1)} %get-tuple-element.219, s32[1024]{0:T(1024)S(1)} %pad_clamp_fusion.2), kind=kCustom, calls=%fused_computation.1.clone.clone.1 | custom fusion | bytes 11796528 | tf_op jit(solution)/shard_map/while/body/eval_jaxpr/jit(_take)/gather | solution.py:45
  317.0 15.4 %broadcast_select_fusion.3 = (bf16[12,384,5,128]{3,2,1,0:T(8,128)(2,1)}, bf16[12,384,5,128]{3,2,1,0:T(8,128)(2,1)}) fusion(bf16[12,384,5,128]{3,2,1,0:T(8,128)(2,1)} %gather_fusion, pred[12]{0:T(512)(128)(4,1)S(1)} %get-tuple-element.188, bf16[12,384,5,128]{3,2,1,0:T(8,128)(2,1)} %gather_fusion.1), kind=kLoop, calls=%fused_computation.13.clone.1 | loop fusion | flops 5898240 | bytes 23592972 | tf_op jit(solution)/shard_map/while/body/eval_jaxpr/jit(_take)/select_n | solution.py:46
  332.4 20.3 %fusion.40 = f32[5,384,4608]{2,1,0:T(8,128)} fusion(bf16[4608,5,128]{2,1,0:T(8,128)(2,1)} %bitcast.57, bf16[3,384,5,128]{3,1,2,0:T(8,128)(2,1)} %get-tuple-element.218, s32[]{:T(128)} %get-tuple-element.203), kind=kOutput, calls=%fused_computation.15.clone.1 | convolution fusion | flops 2264924160 | bytes 45318656 | tf_op jit(solution)/shard_map/while/body/eval_jaxpr/qhd,khd->hqk/dot_general | solution.py:21
  352.8 36.3 %fusion.41 = (f32[5,384]{1,0:T(8,128)S(1)}, bf16[5,384,4608]{2,1,0:T(8,128)(2,1)}) fusion(f32[5,384,4608]{2,1,0:T(8,128)} %fusion.40, pred[4608]{0:T(1024)(128)(4,1)S(1)} %broadcast_in_dim.94), kind=kOutput, calls=%fused_computation.38.clone.1 | output fusion | flops 70783488 | bytes 53096448 | tf_op jit(solution)/shard_map/while/body/eval_jaxpr/sub | solution.py:26
  389.1 15.1 %fusion.42 = f32[3,384,5,128]{1,3,2,0:T(8,128)S(1)} fusion(f32[3,384,5,128]{1,3,2,0:T(8,128)S(1)} %get-tuple-element.204, s32[]{:T(128)} %get-tuple-element.203, bf16[5,384,4608]{2,1,0:T(8,128)(2,1)} %get-tuple-element.191, bf16[4608,5,128]{2,1,0:T(8,128)(2,1)} %bitcast.58), kind=kOutput, calls=%fused_computation.18.clone.1 | convolution fusion | flops 2264924160 | bytes 24576004 | tf_op jit(solution)/shard_map/while/body/eval_jaxpr/hqk,khd->qhd/dot_general | solution.py:29
  405.6 10.6 %gather_fusion = bf16[12,384,5,128]{3,2,1,0:T(8,128)(2,1)} fusion(bf16[18,384,5,128]{3,2,1,0:T(8,128)(2,1)} %get-tuple-element.216, s32[1024]{0:T(1024)S(1)} %pad_clamp_fusion.2), kind=kCustom, calls=%fused_computation.clone.clone.1 | custom fusion | bytes 11796528 | tf_op jit(solution)/shard_map/while/body/eval_jaxpr/jit(_take)/gather | solution.py:46
  416.2 10.6 %gather_fusion.1 = bf16[12,384,5,128]{3,2,1,0:T(8,128)(2,1)} fusion(bf16[18,384,5,128]{3,2,1,0:T(8,128)(2,1)} %get-tuple-element.219, s32[1024]{0:T(1024)S(1)} %pad_clamp_fusion.2), kind=kCustom, calls=%fused_computation.1.clone.clone.1 | custom fusion | bytes 11796528 | tf_op jit(solution)/shard_map/while/body/eval_jaxpr/jit(_take)/gather | solution.py:45
  426.8 15.4 %broadcast_select_fusion.3 = (bf16[12,384,5,128]{3,2,1,0:T(8,128)(2,1)}, bf16[12,384,5,128]{3,2,1,0:T(8,128)(2,1)}) fusion(bf16[12,384,5,128]{3,2,1,0:T(8,128)(2,1)} %gather_fusion, pred[12]{0:T(512)(128)(4,1)S(1)} %get-tuple-element.188, bf16[12,384,5,128]{3,2,1,0:T(8,128)(2,1)} %gather_fusion.1), kind=kLoop, calls=%fused_computation.13.clone.1 | loop fusion | flops 5898240 | bytes 23592972 | tf_op jit(solution)/shard_map/while/body/eval_jaxpr/jit(_take)/select_n | solution.py:46
  442.2 20.3 %fusion.40 = f32[5,384,4608]{2,1,0:T(8,128)} fusion(bf16[4608,5,128]{2,1,0:T(8,128)(2,1)} %bitcast.57, bf16[3,384,5,128]{3,1,2,0:T(8,128)(2,1)} %get-tuple-element.218, s32[]{:T(128)} %get-tuple-element.203), kind=kOutput, calls=%fused_computation.15.clone.1 | convolution fusion | flops 2264924160 | bytes 45318656 | tf_op jit(solution)/shard_map/while/body/eval_jaxpr/qhd,khd->hqk/dot_general | solution.py:21
  462.6 36.3 %fusion.41 = (f32[5,384]{1,0:T(8,128)S(1)}, bf16[5,384,4608]{2,1,0:T(8,128)(2,1)}) fusion(f32[5,384,4608]{2,1,0:T(8,128)} %fusion.40, pred[4608]{0:T(1024)(128)(4,1)S(1)} %broadcast_in_dim.94), kind=kOutput, calls=%fused_computation.38.clone.1 | output fusion | flops 70783488 | bytes 53096448 | tf_op jit(solution)/shard_map/while/body/eval_jaxpr/sub | solution.py:26
  498.9 15.1 %fusion.42 = f32[3,384,5,128]{1,3,2,0:T(8,128)S(1)} fusion(f32[3,384,5,128]{1,3,2,0:T(8,128)S(1)} %get-tuple-element.204, s32[]{:T(128)} %get-tuple-element.203, bf16[5,384,4608]{2,1,0:T(8,128)(2,1)} %get-tuple-element.191, bf16[4608,5,128]{2,1,0:T(8,128)(2,1)} %bitcast.58), kind=kOutput, calls=%fused_computation.18.clone.1 | convolution fusion | flops 2264924160 | bytes 24576004 | tf_op jit(solution)/shard_map/while/body/eval_jaxpr/hqk,khd->qhd/dot_general | solution.py:29
  515.4 10.6 %gather_fusion = bf16[12,384,5,128]{3,2,1,0:T(8,128)(2,1)} fusion(bf16[18,384,5,128]{3,2,1,0:T(8,128)(2,1)} %get-tuple-element.216, s32[1024]{0:T(1024)S(1)} %pad_clamp_fusion.2), kind=kCustom, calls=%fused_computation.clone.clone.1 | custom fusion | bytes 11796528 | tf_op jit(solution)/shard_map/while/body/eval_jaxpr/jit(_take)/gather | solution.py:46
  526.0 10.6 %gather_fusion.1 = bf16[12,384,5,128]{3,2,1,0:T(8,128)(2,1)} fusion(bf16[18,384,5,128]{3,2,1,0:T(8,128)(2,1)} %get-tuple-element.219, s32[1024]{0:T(1024)S(1)} %pad_clamp_fusion.2), kind=kCustom, calls=%fused_computation.1.clone.clone.1 | custom fusion | bytes 11796528 | tf_op jit(solution)/shard_map/while/body/eval_jaxpr/jit(_take)/gather | solution.py:45
  536.5 15.4 %broadcast_select_fusion.3 = (bf16[12,384,5,128]{3,2,1,0:T(8,128)(2,1)}, bf16[12,384,5,128]{3,2,1,0:T(8,128)(2,1)}) fusion(bf16[12,384,5,128]{3,2,1,0:T(8,128)(2,1)} %gather_fusion, pred[12]{0:T(512)(128)(4,1)S(1)} %get-tuple-element.188, bf16[12,384,5,128]{3,2,1,0:T(8,128)(2,1)} %gather_fusion.1), kind=kLoop, calls=%fused_computation.13.clone.1 | loop fusion | flops 5898240 | bytes 23592972 | tf_op jit(solution)/shard_map/while/body/eval_jaxpr/jit(_take)/select_n | solution.py:46
  551.9 20.3 %fusion.40 = f32[5,384,4608]{2,1,0:T(8,128)} fusion(bf16[4608,5,128]{2,1,0:T(8,128)(2,1)} %bitcast.57, bf16[3,384,5,128]{3,1,2,0:T(8,128)(2,1)} %get-tuple-element.218, s32[]{:T(128)} %get-tuple-element.203), kind=kOutput, calls=%fused_computation.15.clone.1 | convolution fusion | flops 2264924160 | bytes 45318656 | tf_op jit(solution)/shard_map/while/body/eval_jaxpr/qhd,khd->hqk/dot_general | solution.py:21
  572.3 36.3 %fusion.41 = (f32[5,384]{1,0:T(8,128)S(1)}, bf16[5,384,4608]{2,1,0:T(8,128)(2,1)}) fusion(f32[5,384,4608]{2,1,0:T(8,128)} %fusion.40, pred[4608]{0:T(1024)(128)(4,1)S(1)} %broadcast_in_dim.94), kind=kOutput, calls=%fused_computation.38.clone.1 | output fusion | flops 70783488 | bytes 53096448 | tf_op jit(solution)/shard_map/while/body/eval_jaxpr/sub | solution.py:26
  608.6 15.1 %fusion.42 = f32[3,384,5,128]{1,3,2,0:T(8,128)S(1)} fusion(f32[3,384,5,128]{1,3,2,0:T(8,128)S(1)} %get-tuple-element.204, s32[]{:T(128)} %get-tuple-element.203, bf16[5,384,4608]{2,1,0:T(8,128)(2,1)} %get-tuple-element.191, bf16[4608,5,128]{2,1,0:T(8,128)(2,1)} %bitcast.58), kind=kOutput, calls=%fused_computation.18.clone.1 | convolution fusion | flops 2264924160 | bytes 24576004 | tf_op jit(solution)/shard_map/while/body/eval_jaxpr/hqk,khd->qhd/dot_general | solution.py:29
  631.0 25.1 %all_to_all.73 = bf16[8,144,640]{2,1,0:T(8,128)(2,1)S(1)} all-to-all(bf16[8,144,640]{2,1,0:T(8,128)(2,1)} %all_to_all.65), channel_id=1, replica_groups=mesh['blk'=16,'uly'=8] {'uly'}, dimensions={0} | all-to-all | bytes 2949120 | tf_op jit(solution)/shard_map/all_to_all | solution.py:79
  (57 shorter events, 88.0 us)
Async XLA Ops:
  0.0 102.8 %copy-start = (s32[48,12]{0,1:T(8,128)S(1)}, s32[48,12]{0,1:T(8,128)}, u32[]{:S(2)}) copy-start(s32[48,12]{0,1:T(8,128)} %param.12) | copy-start | bytes 6916
  3.7 42.5 %all-to-all-start.2 = ((bf16[288,8,640]{2,0,1:T(8,128)(2,1)}), bf16[288,8,640]{2,0,1:T(8,128)(2,1)S(1)}, u32[]{:S(2)}, u32[]{:S(2)}) async-start(bf16[288,8,640]{2,0,1:T(8,128)(2,1)} %bitcast.66), calls=%async_computation.2 | async-start | bytes 5898240 | tf_op jit(solution)/shard_map/all_to_all | solution.py:56
  10.6 92.4 %copy-start.4 = (s32[48]{0:T(128)S(1)}, s32[48]{0:T(128)}, u32[]{:S(2)}) copy-start(s32[48]{0:T(128)} %param.13) | copy-start | bytes 580
  46.2 1.6 copy-start.2
  47.8 41.7 %all-to-all-start = ((bf16[288,8,640]{2,0,1:T(8,128)(2,1)}), bf16[288,8,640]{2,0,1:T(8,128)(2,1)S(1)}, u32[]{:S(2)}, u32[]{:S(2)}) async-start(bf16[288,8,640]{2,0,1:T(8,128)(2,1)} %bitcast.65), calls=%async_computation | async-start | bytes 5898240 | tf_op jit(solution)/shard_map/all_to_all | solution.py:57
  52.5 185.4 %collective-permute-start.2 = (bf16[2304,640]{1,0:T(8,128)(2,1)}, bf16[2304,640]{1,0:T(8,128)(2,1)}, u32[]{:S(2)}, u32[]{:S(2)}) collective-permute-start(bf16[2304,640]{1,0:T(8,128)(2,1)} %bitcast.62), channel_id=1, source_target_pairs={{0,8},{8,16},{16,24},{24,32},{32,40},{40,48},{48,56},{56,64},{64,7... | collective-permute-start | bytes 8847368 | tf_op jit(solution)/shard_map/ppermute | solution.py:15
  54.4 183.5 %collective-permute-start.3 = (bf16[2304,640]{1,0:T(8,128)(2,1)}, bf16[2304,640]{1,0:T(8,128)(2,1)}, u32[]{:S(2)}, u32[]{:S(2)}) collective-permute-start(bf16[2304,640]{1,0:T(8,128)(2,1)} %bitcast.63), channel_id=1, source_target_pairs={{8,0},{16,8},{24,16},{32,24},{40,32},{48,40},{56,48},{64,56},{72,6... | collective-permute-start | bytes 8847368 | tf_op jit(solution)/shard_map/ppermute | solution.py:15
  89.4 177.3 %collective-permute-start = (bf16[2304,640]{1,0:T(8,128)(2,1)S(1)}, bf16[2304,640]{1,0:T(8,128)(2,1)}, u32[]{:S(2)}, u32[]{:S(2)}) collective-permute-start(bf16[2304,640]{1,0:T(8,128)(2,1)S(1)} %bitcast.59), channel_id=1, source_target_pairs={{0,8},{8,16},{16,24},{24,32},{32,40},{40,48},{48,56},{56,64},{64,7... | collective-permute-start | bytes 8847368 | tf_op jit(solution)/shard_map/ppermute | solution.py:15
  91.4 175.4 %collective-permute-start.1 = (bf16[2304,640]{1,0:T(8,128)(2,1)S(1)}, bf16[2304,640]{1,0:T(8,128)(2,1)}, u32[]{:S(2)}, u32[]{:S(2)}) collective-permute-start(bf16[2304,640]{1,0:T(8,128)(2,1)S(1)} %bitcast.60), channel_id=1, source_target_pairs={{8,0},{16,8},{24,16},{32,24},{40,32},{48,40},{56,48},{64,56},{72,6... | collective-permute-start | bytes 8847368 | tf_op jit(solution)/shard_map/ppermute | solution.py:15
  98.5 132.0 %all-to-all-start.1 = ((bf16[144,8,640]{2,0,1:T(8,128)(2,1)}), bf16[144,8,640]{2,0,1:T(8,128)(2,1)}, u32[]{:S(2)}, u32[]{:S(2)}) async-start(bf16[144,8,640]{2,0,1:T(8,128)(2,1)} %bitcast.67), calls=%async_computation.1 | async-start | bytes 2949120 | tf_op jit(solution)/shard_map/all_to_all | solution.py:55
  274.2 20.2 %copy-start.3 = (f32[3,384,5,128]{1,3,2,0:T(8,128)S(1)}, f32[3,384,5,128]{1,3,2,0:T(8,128)}, u32[]{:S(2)}) copy-start(f32[3,384,5,128]{1,3,2,0:T(8,128)} %custom-call.4) | copy-start | bytes 8847364
  623.7 33.6 %copy-start.1 = (s32[48,12]{0,1:T(8,128)S(1)}, s32[48,12]{0,1:T(8,128)}, u32[]{:S(2)}) copy-start(s32[48,12]{0,1:T(8,128)} %param.12) | copy-start | bytes 6916
where the time goes:
time: 660 us; the launch traced here: 657 us
  waiting for transfers between devices  190 us (29%)
  other arithmetic  175 us (27%)
  local copies, waits for them, and re-layouts  132 us (20%)
  matrix products  106 us (16%)
  starting transfers between devices  28.9 us (4%)
  blocking collectives  25.1 us (4%)
    all_to_all x1, waiting for transfers between devices, per_device(): lax.all_to_all(queries, 'uly', split_axis=1, concat_axis=0, tiled=True)  127 us
    sub x3, other arithmetic, score_tile(): scores - peak[:, :, None]  109 us
    dot_general x3, matrix products, score_tile(): jnp.einsum('qhd,khd->hqk', query_tile, key_rows, preferred_element_type=j...  60.9 us
    select_n x3, other arithmetic, one_tile(): jnp.take(value_tiles, safe_ids, axis=0)  46.2 us
    dot_general x3, matrix products, score_tile(): jnp.einsum('hqk,khd->qhd', rounded, value_rows, preferred_element_type=jn...  45.2 us
    all_to_all x1, waiting for transfers between devices, per_device(): lax.all_to_all(keys, 'uly', split_axis=1, concat_axis=0, tiled=True)  31.8 us
    gather x3, local copies, waits for them, and re-layouts, one_tile(): jnp.take(key_tiles, safe_ids, axis=0).reshape(MAXT * TILE, heads_local, HD)  31.8 us
    gather x3, local copies, waits for them, and re-layouts, one_tile(): jnp.take(value_tiles, safe_ids, axis=0)  31.7 us
  transfers between devices with their start and end apart: 7, of which 3 were waited for; matrix products, arithmetic and copies ran while one was open for 7% of the time, Pallas kernels for 0%

commit v1 on v0

v1 whole, which is shorter than its diff:
```python
import functools

import jax
import jax.numpy as jnp
from jax import lax
from jax.experimental import pallas as pl
from jax.experimental.pallas import tpu as pltpu
from jax.sharding import PartitionSpec as P

HD = 128
TILE = 384
FT = 3
MAXT = 12
HEADS = 40
BLOCK = 2304
HALF = 1152
KROWS = 288
QROWS = 144
MAIN = 32
LEFT = 5 * BLOCK + HALF
KV_ROWS = LEFT + 3 * BLOCK + HALF
UNITS = 6
MESH = pl.DeviceIdType.MESH
OFFSETS = [(dx, (k - dx) % 4) for k in (1, 3, 2, 0) for dx in (1, 3, 2, 0)]


class Place:
    def __init__(self):
        blk, uly = lax.axis_index("blk"), lax.axis_index("uly")
        self.z, self.b, self.u = blk // 4, blk % 4, uly
        self.c = blk % 2
        self.xl = self.b // 2
        self.x = (uly // 4) * 2 + self.xl
        self.y = uly % 4
        self.chip = self.x * 4 + self.y
        self.odd = (self.x + self.y) % 2
        self.heavy = self.odd == 0

    def at(self, z, x, y, c):
        return (z * 4 + (x % 2) * 2 + c, (x // 2) * 4 + y)


def greet(me):
    barrier = pltpu.get_barrier_semaphore()

    def hello(z, x, y, c):
        pl.semaphore_signal(barrier, inc=1, device_id=me.at(z, x, y, c), device_id_type=MESH)

    for dx, dy in OFFSETS:
        x, y = (me.x + dx) % 4, (me.y + dy) % 4
        if (dx, dy) != (0, 0):
            hello(me.z, x, y, me.c)
        hello(me.z, x, y, 1 - me.c)
    return barrier, hello


def exchange_kernel(q, k, v, qo, ko, vo, send, left_send, main_in, left_in, q_in, fwd_send, fwd_in):
    me = Place()
    barrier, hello = greet(me)

    @pl.when(me.z > 0)
    def _():
        hello(me.z - 1, me.x, me.y, 0)
        hello(me.z - 1, me.x, me.y, 1)

    @pl.when(me.z < 3)
    def _():
        hello(me.z + 1, me.x, me.y, 0)
        hello(me.z + 1, me.x, me.y, 1)

    above = jnp.where(me.z < 3, 2, 0)
    below = jnp.where(me.z > 0, 2, 0)
    pl.semaphore_wait(barrier, 31 + above + below)

    def columns(head):
        return pl.ds(pl.multiple_of(head * HD, HD), HD)

    def rows(start, size):
        return pl.ds(pl.multiple_of(start, 16), size)

    def scatter(source, target, size, main_row, left_row, s, main_sem, left_sem):
        for dx, dy in OFFSETS:
            x, y = (me.x + dx) % 4, (me.y + dy) % 4
            for dc in (0, 1):
                c = me.c if dc == 0 else 1 - me.c
                src = source.at[:, columns((x * 4 + y) * 2 + c)]
                dst = target.at[rows(main_row, size), :]
                if (dx, dy, dc) == (0, 0, 0):
                    pltpu.make_async_copy(src, dst, main_sem).start()
                else:
                    pltpu.make_async_remote_copy(
                        src, dst, send.at[s], main_sem, device_id=me.at(me.z, x, y, c), device_id_type=MESH
                    ).start()
        for k2 in (2, 0):
            for dx in (1, 3, 2, 0):
                x = (me.x + dx) % 4
                y = (me.y + me.odd + k2 + 4 - dx) % 4
                src = source.at[:, columns(MAIN + (x * 4 + y) // 2)]
                dst = target.at[rows(left_row, size), :]

                def away():
                    pltpu.make_async_remote_copy(
                        src, dst, left_send.at[s], left_sem, device_id=me.at(me.z, x, y, me.xl), device_id_type=MESH
                    ).start()

                if (k2, dx) != (0, 0):
                    away()
                else:
                    own = jnp.logical_and(me.heavy, me.xl == me.c)

                    @pl.when(own)
                    def _():
                        pltpu.make_async_copy(src, dst, left_sem).start()

                    @pl.when(jnp.logical_not(own))
                    def _():
                        away()

    e = me.b % 2
    kv_main = BLOCK * (1 + me.b) + me.u * KROWS
    kv_left = LEFT + BLOCK * (1 + e) + me.u * KROWS

    def arrived(target, start, size, sem):
        ref = target.at[pl.ds(start, size), :]
        pltpu.make_async_copy(ref, ref, sem).wait()

    def forward(i, target, src, dst, size, device):
        return pltpu.make_async_remote_copy(
            target.at[pl.ds(src, size), :], target.at[pl.ds(dst, size), :],
            fwd_send.at[i], fwd_in.at[i], device_id=device, device_id_type=MESH,
        )

    not_last, not_first = me.z < 3, me.z > 0
    heavy = me.heavy
    up_left = jnp.logical_and(heavy, jnp.logical_or(me.c == 0, not_last))
    down_left = jnp.logical_and(heavy, jnp.logical_or(me.c == 1, not_first))
    from_prev = jnp.logical_and(heavy, jnp.logical_or(me.c == 1, not_first))
    from_next = jnp.logical_and(heavy, jnp.logical_or(me.c == 0, not_last))

    def copies(a, target):
        return (
            forward(4 * a, target, BLOCK * 4, 0, BLOCK, me.at(me.z + 1, me.x, me.y, me.c)),
            forward(4 * a + 1, target, BLOCK, 5 * BLOCK, HALF, me.at(me.z - 1, me.x, me.y, me.c)),
            forward(4 * a + 2, target, LEFT + 2 * BLOCK, LEFT, BLOCK, me.at(me.z + me.c, me.x, me.y, 1 - me.c)),
            forward(4 * a + 3, target, LEFT + BLOCK, LEFT + 3 * BLOCK, HALF,
                    me.at(me.z - 1 + me.c, me.x, me.y, 1 - me.c)),
        )

    def pass_on(a, target):
        up, down, left_up, left_down = copies(a, target)
        arrived(target, BLOCK * 4, BLOCK, main_in.at[4 * a + 3])

        @pl.when(not_last)
        def _():
            up.start()

        arrived(target, BLOCK, BLOCK, main_in.at[4 * a])

        @pl.when(not_first)
        def _():
            down.start()

        @pl.when(heavy)
        def _():
            arrived(target, LEFT + 2 * BLOCK, BLOCK, left_in.at[2 * a + 1])

            @pl.when(up_left)
            def _():
                left_up.start()

            arrived(target, LEFT + BLOCK, BLOCK, left_in.at[2 * a])

            @pl.when(down_left)
            def _():
                left_down.start()

    scatter(k, ko, KROWS, kv_main, kv_left, 0, main_in.at[me.b], left_in.at[e])
    scatter(v, vo, KROWS, kv_main, kv_left, 1, main_in.at[4 + me.b], left_in.at[2 + e])
    pass_on(0, ko)
    scatter(q, qo, QROWS, HALF * me.b + me.u * QROWS, HALF * (4 + e) + me.u * QROWS, 2, q_in.at[0], q_in.at[1])
    pass_on(1, vo)

    for a, target in ((0, ko), (1, vo)):
        arrived(target, BLOCK * 2, BLOCK, main_in.at[4 * a + 1])
        arrived(target, BLOCK * 3, BLOCK, main_in.at[4 * a + 2])
    arrived(qo, 0, 4 * HALF, q_in.at[0])

    @pl.when(heavy)
    def _():
        arrived(qo, 4 * HALF, 2 * HALF, q_in.at[1])

    for a, target in ((0, ko), (1, vo)):
        up, down, left_up, left_down = copies(a, target)
        for copy, sent, got in (
            (up, not_last, not_first),
            (down, not_first, not_last),
            (left_up, up_left, from_prev),
            (left_down, down_left, from_next),
        ):
            @pl.when(sent)
            def _():
                copy.wait_send()

            @pl.when(got)
            def _():
                copy.wait_recv()

    own = jnp.logical_and(heavy, me.xl == me.c)
    for s, source in enumerate((k, v, q)):
        def sent(n, sem):
            ref = source.at[:, pl.ds(0, n * HD)]
            pltpu.make_async_copy(ref, ref, sem).wait()

        sent(31, send.at[s])

        @pl.when(own)
        def _():
            sent(7, left_send.at[s])

        @pl.when(jnp.logical_not(own))
        def _():
            sent(8, left_send.at[s])


def exchange(q, k, v):
    anywhere = pl.BlockSpec(memory_space=pl.ANY)
    dma = pltpu.SemaphoreType.DMA
    return pl.pallas_call(
        exchange_kernel,
        out_shape=(
            jax.ShapeDtypeStruct((UNITS * HALF, HD), jnp.bfloat16),
            jax.ShapeDtypeStruct((KV_ROWS, HD), jnp.bfloat16),
            jax.ShapeDtypeStruct((KV_ROWS, HD), jnp.bfloat16),
        ),
        in_specs=[anywhere] * 3,
        out_specs=(anywhere,) * 3,
        scratch_shapes=[dma((3,)), dma((3,)), dma((8,)), dma((4,)), dma((2,)), dma((8,)), dma((8,))],
        compiler_params=pltpu.CompilerParams(collective_id=0, has_side_effects=True),
        name="exchange",
    )(q, k, v)


def attend_kernel(lists, counts, place, q, k, v, out):
    unit, t = pl.program_id(0), pl.program_id(1)
    z, c, heavy = place[0], place[1], place[2]
    shared = unit >= 4
    block = 4 * z + jnp.where(shared, 2 * c + unit - 4, unit)
    tile = block * FT + t
    first = jnp.where(shared, 33 - (4 * z + 2 * c - 1) * 6, -(4 * z - 1) * 6)
    scale = HD ** (-0.5) * 1.4426950408889634

    @pl.when(jnp.logical_or(unit < 4, heavy > 0))
    def _():
        query = q[...]
        ones = jnp.ones((TILE, HD), jnp.bfloat16)

        def scores(m):
            row = pl.multiple_of((lists[tile, m] + first) * TILE, TILE)
            s = lax.dot_general(
                query, k[pl.ds(row, TILE), :], (((1,), (1,)), ((), ())), preferred_element_type=jnp.float32
            )
            return s, row

        def weighted(s, peak, row):
            w = jnp.exp2((s - peak) * scale).astype(jnp.bfloat16)
            both = jnp.concatenate([v[pl.ds(row, TILE), :], ones], axis=1)
            return jnp.dot(w, both, preferred_element_type=jnp.float32)

        s, row = scores(0)
        peak = jnp.max(s, axis=1, keepdims=True)
        total = weighted(s, peak, row)

        def step(m, carry):
            peak, total = carry
            s, row = scores(m)
            higher = jnp.maximum(peak, jnp.max(s, axis=1, keepdims=True))
            return higher, total * jnp.exp2((peak - higher) * scale) + weighted(s, higher, row)

        peak, total = lax.fori_loop(1, counts[tile], step, (peak, total))
        out[...] = (total[:, :HD] / total[:, HD:]).astype(jnp.bfloat16)


def attend(lists, counts, place, q, k, v):
    whole = pl.BlockSpec((KV_ROWS, HD), lambda unit, t, *_: (0, 0))
    tile = pl.BlockSpec((TILE, HD), lambda unit, t, *_: (unit * FT + t, 0))
    return pl.pallas_call(
        attend_kernel,
        out_shape=jax.ShapeDtypeStruct((UNITS * HALF, HD), jnp.bfloat16),
        grid_spec=pltpu.PrefetchScalarGridSpec(
            num_scalar_prefetch=3,
            grid=(UNITS, FT),
            in_specs=[tile, whole, whole],
            out_specs=tile,
        ),
        compiler_params=pltpu.CompilerParams(vmem_limit_bytes=48 * 1024 * 1024),
        name="attend",
    )(lists, counts, place, q, k, v)


def collect_kernel(a, out, send, left_send, arrive):
    me = Place()
    barrier, _ = greet(me)
    pl.semaphore_wait(barrier, 31)

    def one(row, head, x, y, c, local, sem):
        src = a.at[pl.ds(pl.multiple_of(row, 16), QROWS), :]
        dst = out.at[:, pl.ds(pl.multiple_of(head * HD, HD), HD)]
        if local:
            pltpu.make_async_copy(src, dst, arrive).start()
        else:
            pltpu.make_async_remote_copy(
                src, dst, sem, arrive, device_id=me.at(me.z, x, y, c), device_id_type=MESH
            ).start()

    for dx, dy in OFFSETS:
        x, y = (me.x + dx) % 4, (me.y + dy) % 4
        b, u = x % 2, (x // 2) * 4 + y
        for dc in (0, 1):
            c = me.c if dc == 0 else 1 - me.c
            one((2 * b + c) * HALF + u * QROWS, me.chip * 2 + me.c, x, y, c, (dx, dy, dc) == (0, 0, 0), send)

    @pl.when(me.heavy)
    def _():
        for dh, dy in ((0, 1), (1, 3), (1, 2), (0, 3), (1, 1), (0, 2), (1, 0), (0, 0)):
            x = (me.x // 2 * 2 + 2 * dh + me.c) % 4
            y = (me.y + dy) % 4
            u = (x // 2) * 4 + y
            for dc in (0, 1):
                c = me.c if dc == 0 else 1 - me.c
                row, head = (4 + c) * HALF + u * QROWS, MAIN + me.chip // 2
                if (dh, dy, dc) != (0, 0, 0):
                    one(row, head, x, y, c, False, left_send)
                else:
                    @pl.when(me.xl == me.c)
                    def _():
                        one(row, head, x, y, c, True, left_send)

                    @pl.when(me.xl != me.c)
                    def _():
                        one(row, head, x, y, c, False, left_send)

    pltpu.make_async_copy(out, out, arrive).wait()

    def sent(n, sem):
        ref = a.at[pl.ds(0, n * QROWS), :]
        pltpu.make_async_copy(ref, ref, sem).wait()

    sent(31, send)

    @pl.when(jnp.logical_and(me.heavy, me.xl == me.c))
    def _():
        sent(15, left_send)

    @pl.when(jnp.logical_and(me.heavy, me.xl != me.c))
    def _():
        sent(16, left_send)


def collect(a):
    dma = pltpu.SemaphoreType.DMA
    return pl.pallas_call(
        collect_kernel,
        out_shape=jax.ShapeDtypeStruct((QROWS, HEADS * HD), jnp.bfloat16),
        in_specs=[pl.BlockSpec(memory_space=pl.ANY)],
        out_specs=pl.BlockSpec(memory_space=pl.ANY),
        scratch_shapes=[dma, dma, dma],
        compiler_params=pltpu.CompilerParams(collective_id=1, has_side_effects=True),
        name="collect",
    )(a)


def per_device(queries, keys, values, tile_lists, tile_counts):
    me = Place()
    place = jnp.stack([me.z, me.c, 1 - me.odd]).astype(jnp.int32)
    q, k, v = exchange(queries, keys, values)
    return collect(attend(tile_lists, tile_counts, place, q, k, v))


def solution(mesh):
    placed = (P(("blk", "uly"), None), P(("blk", "uly"), None), P(("blk", "uly"), None), P(), P())
    return jax.shard_map(
        per_device, mesh=mesh, in_specs=placed, out_specs=P(("blk", "uly"), None), check_vma=False
    )
```

time: 660 us -> 247 us (0.37)
  Pallas kernels: 0 us -> 240 us
  waiting for transfers between devices: 190 us -> 0 us
  other arithmetic: 175 us -> 0.08 us
  local copies, waits for them, and re-layouts: 132 us -> 6.06 us
  matrix products: 106 us -> 0 us
  starting transfers between devices: 28.9 us -> 0 us
  blocking collectives: 25.1 us -> 0 us
    pallas_call x0 -> x3, Pallas kernels: none -> 240 us  [the longest x1 107 us: exchange(): pl.pallas_call(exchange_kernel, out_shape=(jax.ShapeDtypeStruct((UNITS *...]
    all_to_all x3 -> x0, waiting for transfers between devices: 190 us -> none  [the longest x1 127 us: per_device(): lax.all_to_all(queries, 'uly', split_axis=1, concat_axis=0, tiled=True)]
    sub x4 -> x0, other arithmetic: 109 us -> none  [the longest x3 109 us: score_tile(): scores - peak[:, :, None]]
    dot_general x6 -> x0, matrix products: 106 us -> none  [the longest x3 60.9 us: score_tile(): jnp.einsum('qhd,khd->hqk', query_tile, key_rows, preferred_element_type=j...]
    gather x6 -> x0, local copies, waits for them, and re-layouts: 63.5 us -> none  [the longest x3 31.8 us: one_tile(): jnp.take(key_tiles, safe_ids, axis=0).reshape(MAXT * TILE, heads_local, HD)]
    select_n x3 -> x0, other arithmetic: 46.2 us -> none  [one_tile(): jnp.take(value_tiles, safe_ids, axis=0)]
    reshape x3 -> x0, local copies, waits for them, and re-layouts: 44.6 us -> none  [the longest x1 20.2 us: per_device(): value_tiles = value_rows_all.reshape(-1, TILE, heads_local, HD)]
    all_to_all x1 -> x0, blocking collectives: 25.1 us -> none  [per_device(): lax.all_to_all(attended, 'uly', split_axis=0, concat_axis=1, tiled=True)]
  transfers between devices with their start and end apart: 7 -> 0, of which waited for: 3 -> 0; matrix products, arithmetic and copies ran while one was open for 7% -> 0% of each run, Pallas kernels for 0% -> 0%
where the time goes in v1:
time: 247 us; the launch traced here: 246 us
  Pallas kernels  240 us (97%)
  local copies, waits for them, and re-layouts  6.06 us (2%)
    pallas_call x1, Pallas kernels, exchange(): pl.pallas_call(exchange_kernel, out_shape=(jax.ShapeDtypeStruct((UNITS *...  107 us
    pallas_call x1, Pallas kernels, attend(): pl.pallas_call(attend_kernel, out_shape=jax.ShapeDtypeStruct((UNITS * HAL...  104 us
    pallas_call x1, Pallas kernels, collect(): pl.pallas_call(collect_kernel, out_shape=jax.ShapeDtypeStruct((QROWS, HEA...  29 us
    unnamed x8, local copies, waits for them, and re-layouts  6.06 us

profile of v1, /device:TPU:64, one launch (start us, length us, event | category | flops | bytes accessed | tf_op | source)
XLA Modules:
  0.0 246.2 jit_solution(16294025177037589954)
XLA Ops:
  0.0 0.1 pad_add_fusion.place
  0.1 0.8 copy.6.lists
  0.9 0.0 copy-start.2
  0.9 107.5 %exchange.1 = (bf16[6912,128]{1,0:T(8,128)(2,1)}, bf16[20736,128]{1,0:T(8,128)(2,1)}, bf16[20736,128]{1,0:T(8,128)(2,1)}) custom-call(bf16[144,5120]{1,0:T(8,128)(2,1)} %q.1, bf16[288,5120]{1,0:T(8,128)(2,1)} %k.1, bf16[288,5120]{1,0:T(8,128)(2,1)} %v.1), custom_call_target="tpu_custom_call" | custom-call | tf_op jit(solution)/shard_map/exchange/pallas_call | solution.py:228
  108.3 0.0 copy-done.2
  108.3 0.0 copy-start.1
  108.4 1.5 copy-done.1
  109.8 103.5 %attend.1.a = bf16[6912,128]{1,0:T(8,128)(2,1)S(1)} custom-call(s32[48,12]{1,0:T(8,128)S(1)} %copy.6.lists, s32[48]{0:T(128)S(1)} %copy-done.2, s32[3]{0:T(128)S(1)} %pad_add_fusion.place, bf16[6912,128]{1,0:T(8,128)(2,1)S(1)} %copy-done.1, bf16[20736,128]{1,0:T(8,128)(2,1)} %get-tuple-element.9.k, bf16[20736,128]{1,0:T(8,128)(2,1)} %get-tuple-element.10.v), custom_call_target="tpu_custom_call" | custom-call | tf_op jit(solution)/shard_map/attend/pallas_call | solution.py:286
  213.4 0.0 copy-start
  213.4 1.2 copy-done
  214.6 29.0 %collect.1 = bf16[144,5120]{1,0:T(8,128)(2,1)} custom-call(bf16[6912,128]{1,0:T(8,128)(2,1)} %copy-done), custom_call_target="tpu_custom_call" | custom-call | tf_op jit(solution)/shard_map/collect/pallas_call | solution.py:361
  243.6 2.6 %copy.8 = bf16[144,5120]{1,0:T(8,128)(2,1)} copy(bf16[144,5120]{1,0:T(8,128)(2,1)} %collect.1) | data formatting | bytes 2949120
Async XLA Ops:
  0.9 107.5 %copy-start.2 = (s32[48]{0:T(128)S(1)}, s32[48]{0:T(128)}, u32[]{:S(2)}) copy-start(s32[48]{0:T(128)} %counts.1) | copy-start | bytes 580
  108.3 1.5 copy-start.1
  213.4 1.2 copy-start

commit v2 on v0

v2 whole, which is shorter than its diff:
```python
import functools

import jax
import jax.numpy as jnp
from jax import lax
from jax.experimental import pallas as pl
from jax.experimental.pallas import tpu as pltpu
from jax.sharding import PartitionSpec as P

HD = 128
TILE = 384
FT = 3
MAXT = 12
HEADS = 40
BLOCK = 2304
HALF = 1152
KROWS = 288
QROWS = 144
MAIN = 32
PAIR = 3 * BLOCK + HALF
ONE = 2 * BLOCK + HALF
VROWS = HD + 16
G = 2
GROUPS = MAXT // G
LOG2_SCALE = HD ** (-0.5) * 1.4426950408889634
FAR = 1e30
MESH = pl.DeviceIdType.MESH
OFFSETS = [(dx, (k - dx) % 4) for k in (1, 3, 2, 0) for dx in (1, 3, 2, 0)]
PAIR_OFFSETS = ((1, 0), (2, 1), (3, 0), (0, 1), (1, 1), (2, 0), (3, 1), (0, 0))
HALF_OFFSETS = ((0, 1), (1, 3), (1, 2), (0, 3), (1, 1), (0, 2), (1, 0), (0, 0))


def rows(start, size):
    return pl.ds(pl.multiple_of(start, 16), size)


def columns(head):
    return pl.ds(pl.multiple_of(head * HD, HD), HD)


def arrived(ref, sem):
    pltpu.make_async_copy(ref, ref, sem).wait()


def kernel(
    lists, counts, q, k, v, out,
    qa, qb, ql, ka, kb, kl, va, vb, vl, done, kt, vt, qt, s0, s1, acc,
    send, got, q_got, fwd_send, fwd_got, halo_send, halo_got, out_send, out_got,
):
    blk, u = lax.axis_index("blk"), lax.axis_index("uly")
    z, b, c = blk // 4, blk % 4, blk % 2
    xl = b // 2
    x, y = (u // 4) * 2 + xl, u % 4
    chip = x * 4 + y
    quarter = (y % 2) * 2 + c
    not_first, not_last = z > 0, z < 3
    mine = xl == c
    mine_l = xl == y % 2
    no = jnp.logical_not
    both = jnp.logical_and
    either = jnp.logical_or

    def at(z, x, y, c):
        return (z * 4 + (x % 2) * 2 + c, (x // 2) * 4 + y)

    def remote(src, dst, send_sem, recv_sem, device):
        return pltpu.make_async_remote_copy(
            src, dst, send_sem, recv_sem, device_id=device, device_id_type=MESH
        )

    barrier = pltpu.get_barrier_semaphore()

    def hello(device):
        pl.semaphore_signal(barrier, inc=1, device_id=device, device_id_type=MESH)

    for dx, dy in OFFSETS:
        there = ((x + dx) % 4, (y + dy) % 4)
        if (dx, dy) != (0, 0):
            hello(at(z, *there, c))
        hello(at(z, *there, 1 - c))
    up = either(c == 0, not_last)
    down = either(c == 1, not_first)

    @pl.when(both(c == 0, not_first))
    def _():
        hello(at(z - 1, x, y, 1))

    @pl.when(both(c == 1, not_last))
    def _():
        hello(at(z + 1, x, y, 0))

    @pl.when(both(quarter == 0, not_first))
    def _():
        for i in range(8):
            hello(at(z - 1, (i // 4) * 2 + 1, i % 4, 1))

    @pl.when(both(quarter == 3, not_last))
    def _():
        for i in range(4):
            hello(at(z + 1, 0, i, 0))

    halo_up = both(b == 3, not_last)
    halo_down = both(both(b == 0, u < 4), not_first)
    pl.semaphore_wait(
        barrier,
        31
        + jnp.where(both(c == 1, not_last), 1, 0)
        + jnp.where(both(c == 0, not_first), 1, 0)
        + jnp.where(halo_up, 8, 0)
        + jnp.where(halo_down, 8, 0),
    )

    e = b % 2

    def scatter(r, source, target, row, size, s, sem):
        for dx, dy in OFFSETS:
            px, py = (x + dx) % 4, (y + dy) % 4
            src = source.at[:, columns((px * 4 + py) * 2 + r)]
            dst = target.at[rows(row, size), :]

            def away():
                remote(src, dst, send.at[s], sem, at(z, px, py, xl)).start()

            if (dx, dy) != (0, 0):
                away()
            else:
                @pl.when(mine)
                def _():
                    pltpu.make_async_copy(src, dst, sem).start()

                @pl.when(no(mine))
                def _():
                    away()

    def scatter_shared(source, target, row, size, s, sem):
        for dx, dp in PAIR_OFFSETS:
            px, pp = (x + dx) % 4, (y // 2 + dp) % 2
            src = source.at[:, columns(MAIN + px * 2 + pp)]
            dst = target.at[rows(row, size), :]

            def away():
                remote(src, dst, send.at[s], sem, at(z, px, pp * 2 + xl, e)).start()

            if (dx, dp) != (0, 0):
                away()
            else:
                @pl.when(mine_l)
                def _():
                    pltpu.make_async_copy(src, dst, sem).start()

                @pl.when(no(mine_l))
                def _():
                    away()

    sends_prev = either(b == 1, halo_up)
    sends_next = either(both(b == 2, u < 4), halo_down)

    def scatter_halo(source, target, a):
        @pl.when(sends_prev)
        def _():
            up_z, odd = jnp.where(b == 3, 1, 0), jnp.where(b == 1, 1, 0)
            for dx, dp in PAIR_OFFSETS:
                px, pp = (x + dx) % 4, (y // 2 + dp) % 2
                remote(
                    source.at[:, columns(MAIN + px * 2 + pp)], target.at[rows(u * KROWS, KROWS), :],
                    halo_send.at[a], halo_got.at[a], at(z + up_z, px, pp * 2 + odd, 0),
                ).start()

        @pl.when(sends_next)
        def _():
            down_z = jnp.where(b == 0, 1, 0)
            for dx, dp in PAIR_OFFSETS:
                px, pp = (x + dx) % 4, (y // 2 + dp) % 2
                remote(
                    source.at[:, columns(MAIN + px * 2 + pp)],
                    target.at[rows(2 * BLOCK + (u % 4) * KROWS, KROWS), :],
                    halo_send.at[a], halo_got.at[a], at(z - down_z, px, pp * 2 + down_z, 1),
                ).start()

    kv_row, q_row = BLOCK * (1 + e) + u * KROWS, HALF * e + u * QROWS

    def send_k(r, target):
        scatter(r, k, target, kv_row, KROWS, 3 * r, got.at[4 * r + e])

    def send_v(r, target):
        scatter(r, v, target, kv_row, KROWS, 3 * r + 1, got.at[4 * r + 2 + e])

    def send_q(r, target):
        scatter(r, q, target, q_row, QROWS, 3 * r + 2, q_got.at[r])

    def halos(i, target):
        return (
            remote(
                target.at[pl.ds(2 * BLOCK, BLOCK), :], target.at[pl.ds(0, BLOCK), :],
                fwd_send.at[2 * i], fwd_got.at[2 * i], at(z + c, x, y, 1 - c),
            ),
            remote(
                target.at[pl.ds(BLOCK, HALF), :], target.at[pl.ds(3 * BLOCK, HALF), :],
                fwd_send.at[2 * i + 1], fwd_got.at[2 * i + 1], at(z - 1 + c, x, y, 1 - c),
            ),
        )

    from_prev, from_next = either(c == 1, not_first), either(c == 0, not_last)

    def pass_on(i, target):
        to_up, to_down = halos(i, target)
        arrived(target.at[pl.ds(2 * BLOCK, BLOCK), :], got.at[2 * i + 1])

        @pl.when(up)
        def _():
            to_up.start()

        arrived(target.at[pl.ds(BLOCK, BLOCK), :], got.at[2 * i])

        @pl.when(down)
        def _():
            to_down.start()

    def halos_in(i, target):
        to_up, to_down = halos(i, target)

        @pl.when(from_prev)
        def _():
            to_up.wait_recv()

        @pl.when(from_next)
        def _():
            to_down.wait_recv()

    def halos_sent(i, target):
        to_up, to_down = halos(i, target)

        @pl.when(up)
        def _():
            to_up.wait_send()

        @pl.when(down)
        def _():
            to_down.wait_send()

    def shared_halo(a, target):
        return (
            remote(
                target.at[pl.ds(BLOCK, BLOCK), :], target.at[pl.ds(0, BLOCK), :],
                fwd_send.at[8 + a], fwd_got.at[8 + a], at(z, x, y, 1),
            ),
            remote(
                target.at[pl.ds(BLOCK, HALF), :], target.at[pl.ds(2 * BLOCK, HALF), :],
                fwd_send.at[8 + a], fwd_got.at[8 + a], at(z, x, y, 0),
            ),
        )

    def shared_pass_on(a, target):
        to_other, to_first = shared_halo(a, target)
        arrived(target.at[pl.ds(BLOCK, BLOCK), :], got.at[8 + a])

        @pl.when(c == 0)
        def _():
            to_other.start()

        @pl.when(c == 1)
        def _():
            to_first.start()

    def shared_in(a, target):
        to_other, to_first = shared_halo(a, target)

        @pl.when(both(c == 0, either(quarter == 2, not_first)))
        def _():
            arrived(target.at[pl.ds(0, BLOCK), :], halo_got.at[a])

        @pl.when(both(c == 1, either(quarter == 1, not_last)))
        def _():
            arrived(target.at[pl.ds(2 * BLOCK, HALF), :], halo_got.at[a])

        @pl.when(c == 0)
        def _():
            to_other.wait_send()
            to_first.wait_recv()

        @pl.when(c == 1)
        def _():
            to_first.wait_send()
            to_other.wait_recv()

    def lay_out(keys, values, tiles):
        def one(t, carry):
            row = pl.ds(pl.multiple_of(t * TILE, TILE), TILE)
            kt[t] = keys[row, :]
            vt[t, 0:HD, :] = values[row, :].T
            return carry

        lax.fori_loop(0, tiles, one, 0)

    def attend(queries, query_row, block, first_block, done_row, tiles):
        def scale(t, carry):
            row = pl.multiple_of(query_row + t * TILE, TILE)
            query = queries[pl.ds(row, TILE), :].astype(jnp.float32).T * LOG2_SCALE
            high = query.astype(jnp.bfloat16)
            qt[t, 0:HD, :] = high
            qt[t, HD:2 * HD, :] = (query - high.astype(jnp.float32)).astype(jnp.bfloat16)
            return carry

        lax.fori_loop(0, FT, scale, 0)
        first = first_block * 6

        def place(tile, m):
            return jnp.clip(lists[tile, m] - first, 0, tiles - 1)

        def scores(buffer, t, g):
            tile = block * FT + t
            top = None
            for j in range(G):
                key = kt[place(tile, g * G + j)]
                s = jnp.dot(jnp.concatenate([key, key], axis=1), qt[t], preferred_element_type=jnp.float32)
                buffer[j * TILE:(j + 1) * TILE, :] = s
                t_top = jnp.max(s, axis=0, keepdims=True)
                top = t_top if top is None else jnp.maximum(top, t_top)
            return top

        def weigh(buffer, t, g, peak):
            tile = block * FT + t
            total = None
            for j in range(G):
                m = g * G + j
                shift = peak + jnp.maximum(m + 1 - counts[tile], 0).astype(jnp.float32) * FAR
                w = jnp.exp2(buffer[j * TILE:(j + 1) * TILE, :] - shift).astype(jnp.bfloat16)
                part = jnp.dot(vt[place(tile, m)], w, preferred_element_type=jnp.float32)
                total = part if total is None else total + part
            return total

        def query_tile(t, peak):
            acc[...] = jnp.zeros_like(acc)

            def step(i, peak):
                g = 2 * i
                top = scores(s1, t, g + 1)
                part = weigh(s0, t, g, peak)
                higher = jnp.maximum(peak, top)
                acc[...] = (acc[...] + part) * jnp.exp2(peak - higher)
                after = jnp.where(g + 2 < GROUPS, 0, 1)
                top = scores(s0, jnp.minimum(t + after, FT - 1), (g + 2) * (1 - after))
                part = weigh(s1, t, g + 1, higher)
                highest = jnp.where(after == 1, top, jnp.maximum(higher, top))
                acc[...] = (acc[...] + part) * jnp.where(after == 1, 1.0, jnp.exp2(higher - highest))
                return highest

            peak = lax.fori_loop(0, GROUPS // 2, step, peak)
            total = acc[...]
            row = pl.multiple_of(done_row + t * TILE, TILE)
            done[pl.ds(row, TILE), :] = (total[:HD] / total[HD:HD + 1]).T.astype(jnp.bfloat16)
            return peak

        lax.fori_loop(0, FT, query_tile, scores(s0, 0, 0))

    def give_back(done_row, head, half, core, local, s):
        for dh, dy in HALF_OFFSETS:
            px, py = (x // 2 * 2 + 2 * dh + half) % 4, (y + dy) % 4
            src = done.at[rows(done_row + ((px // 2) * 4 + py) * QROWS, QROWS), :]
            dst = out.at[:, columns(head)]

            def away():
                remote(src, dst, out_send.at[s], out_got, at(z, px, py, core)).start()

            if (dh, dy) != (0, 0):
                away()
            else:
                @pl.when(local)
                def _():
                    pltpu.make_async_copy(src, dst, out_got).start()

                @pl.when(no(local))
                def _():
                    away()

    def unit(queries, r, e):
        attend(queries, e * HALF, 4 * z + 2 * c + e, 4 * z + 2 * c - 1, (2 * r + e) * HALF, PAIR // TILE)
        give_back((2 * r + e) * HALF, chip * 2 + r, c, e, both(mine, c == e), r)

    send_k(0, ka)
    send_v(0, va)
    send_q(0, qa)
    vt[:, HD:VROWS, :] = jnp.ones((vt.shape[0], VROWS - HD, TILE), jnp.bfloat16)
    pass_on(0, ka)
    send_k(1, kb)
    pass_on(1, va)
    send_v(1, vb)
    send_q(1, qb)
    arrived(qa, q_got.at[0])
    halos_in(0, ka)
    halos_in(1, va)
    lay_out(ka, va, PAIR // TILE)
    unit(qa, 0, 0)
    pass_on(2, kb)
    scatter_shared(k, kl, BLOCK + u * KROWS, KROWS, 6, got.at[8])
    scatter_halo(k, kl, 0)
    unit(qa, 0, 1)
    pass_on(3, vb)
    scatter_shared(v, vl, BLOCK + u * KROWS, KROWS, 7, got.at[9])
    scatter_halo(v, vl, 1)
    scatter_shared(q, ql, u * QROWS, QROWS, 8, q_got.at[2])
    arrived(qb, q_got.at[1])
    halos_in(2, kb)
    halos_in(3, vb)
    lay_out(kb, vb, PAIR // TILE)
    unit(qb, 1, 0)
    shared_pass_on(0, kl)
    unit(qb, 1, 1)
    shared_pass_on(1, vl)
    arrived(ql, q_got.at[2])
    shared_in(0, kl)
    shared_in(1, vl)
    lay_out(kl, vl, ONE // TILE)
    attend(ql, 0, 4 * z + quarter, 4 * z + quarter - 1, 4 * HALF, ONE // TILE)
    give_back(4 * HALF, MAIN + chip // 2, y % 2, c, mine_l, 2)

    for i, target in enumerate((ka, va, kb, vb)):
        halos_sent(i, target)

    def sent(source, many, fewer, n, sem):
        for condition, size in ((fewer, n - 1), (no(fewer), n)):
            @pl.when(condition)
            def _():
                arrived(many(source, size), sem)

    def heads(source, n):
        return source.at[:, pl.ds(0, n * HD)]

    def parts(source, n):
        return source.at[pl.ds(0, n * QROWS), :]

    for a, source in enumerate((k, v, q)):
        sent(source, heads, mine, 16, send.at[a])
        sent(source, heads, mine, 16, send.at[3 + a])
        sent(source, heads, mine_l, 8, send.at[6 + a])
    for a, source in enumerate((k, v)):
        @pl.when(either(sends_prev, sends_next))
        def _():
            arrived(heads(source, 8), halo_send.at[a])
    sent(done, parts, mine, 16, out_send.at[0])
    sent(done, parts, mine, 16, out_send.at[1])
    sent(done, parts, mine_l, 8, out_send.at[2])
    arrived(out, out_got)


def per_device(queries, keys, values, tile_lists, tile_counts):
    anywhere = pl.BlockSpec(memory_space=pl.ANY)
    scalars = pl.BlockSpec(memory_space=pltpu.SMEM)
    dma = pltpu.SemaphoreType.DMA

    def held(n):
        return pltpu.VMEM((n, HD), jnp.bfloat16)

    return pl.pallas_call(
        kernel,
        out_shape=jax.ShapeDtypeStruct((QROWS, HEADS * HD), jnp.bfloat16),
        in_specs=[scalars, scalars, anywhere, anywhere, anywhere],
        out_specs=anywhere,
        scratch_shapes=[
            held(2 * HALF), held(2 * HALF), held(HALF),
            held(PAIR), held(PAIR), held(ONE),
            held(PAIR), held(PAIR), held(ONE),
            held(5 * HALF),
            pltpu.VMEM((PAIR // TILE, TILE, HD), jnp.bfloat16),
            pltpu.VMEM((PAIR // TILE, VROWS, TILE), jnp.bfloat16),
            pltpu.VMEM((FT, 2 * HD, TILE), jnp.bfloat16),
            pltpu.VMEM((G * TILE, TILE), jnp.float32),
            pltpu.VMEM((G * TILE, TILE), jnp.float32),
            pltpu.VMEM((VROWS, TILE), jnp.float32),
            dma((9,)), dma((10,)), dma((3,)), dma((10,)), dma((10,)), dma((2,)), dma((2,)), dma((3,)), dma,
        ],
        compiler_params=pltpu.CompilerParams(
            collective_id=0, has_side_effects=True, vmem_limit_bytes=60 * 1024 * 1024
        ),
        name="attention",
    )(tile_lists, tile_counts, queries, keys, values)


def solution(mesh):
    placed = (P(("blk", "uly"), None), P(("blk", "uly"), None), P(("blk", "uly"), None), P(), P())
    return jax.shard_map(
        per_device, mesh=mesh, in_specs=placed, out_specs=P(("blk", "uly"), None), check_vma=False
    )
```

time: 660 us -> 138 us (0.21)
  the two profiles are of different devices: /device:TPU:64 before, /device:TPU:66 now
where the time goes in v2:
time: 138 us
  Pallas kernels  134 us (97%)
  local copies, waits for them, and re-layouts  3.96 us (3%)
    pallas_call x1, Pallas kernels, per_device(): pl.pallas_call(kernel, out_shape=jax.ShapeDtypeStruct((QROWS, HEADS * HD)...  134 us
    unnamed x2, local copies, waits for them, and re-layouts  3.96 us

profile of v2, /device:TPU:66, one launch (start us, length us, event | category | flops | bytes accessed | tf_op | source)
XLA Modules:
  0.0 137.7 jit_solution(16397464582847118710)
XLA Ops:
  0.0 1.4 %copy.6.lists = s32[48,12]{1,0:T(8,128)} copy(s32[48,12]{0,1:T(8,128)} %param.8) | data formatting | bytes 4608 | tf_op args[3]
  1.4 133.7 %attention.1 = bf16[144,5120]{1,0:T(8,128)(2,1)} custom-call(s32[48,12]{1,0:T(8,128)} %copy.6.lists, s32[48]{0:T(128)} %counts.1, bf16[144,5120]{1,0:T(8,128)(2,1)} %q.1, bf16[288,5120]{1,0:T(8,128)(2,1)} %k.1, bf16[288,5120]{1,0:T(8,128)(2,1)} %v.1), custom_call_target="tpu_custom_call" | custom-call | tf_op jit(solution)/shard_map/attention/pallas_call | solution.py:454
  135.1 2.6 %copy.8 = bf16[144,5120]{1,0:T(8,128)(2,1)} copy(bf16[144,5120]{1,0:T(8,128)(2,1)} %attention.1) | data formatting | bytes 2949120

commit v3 on v2

--- a/solution.py
+++ b/solution.py
@@ -20,7 +20,7 @@
 PAIR = 3 * BLOCK + HALF
 ONE = 2 * BLOCK + HALF
 VROWS = HD + 16
-G = 2
+G = 3
 GROUPS = MAXT // G
 LOG2_SCALE = HD ** (-0.5) * 1.4426950408889634
 FAR = 1e30
@@ -43,8 +43,8 @@
 
 
 def kernel(
-    lists, counts, q, k, v, out,
-    qa, qb, ql, ka, kb, kl, va, vb, vl, done, kt, vt, qt, s0, s1, acc,
+    lists_in, counts_in, q, k, v, out,
+    lists, counts, list_sem, qa, qb, ql, ka, kb, kl, va, vb, vl, done, kt, vt, qt, s0, s1, acc, kept, peaks,
     send, got, q_got, fwd_send, fwd_got, halo_send, halo_got, out_send, out_got,
 ):
     blk, u = lax.axis_index("blk"), lax.axis_index("uly")
@@ -52,10 +52,12 @@
     xl = b // 2
     x, y = (u // 4) * 2 + xl, u % 4
     chip = x * 4 + y
-    quarter = (y % 2) * 2 + c
+    side = (y + z) % 2
+    quarter = side * 2 + c
+    outer = jnp.logical_or(quarter == 0, quarter == 3)
     not_first, not_last = z > 0, z < 3
     mine = xl == c
-    mine_l = xl == y % 2
+    mine_l = xl == side
     no = jnp.logical_not
     both = jnp.logical_and
     either = jnp.logical_or
@@ -67,6 +69,11 @@
         return pltpu.make_async_remote_copy(
             src, dst, send_sem, recv_sem, device_id=device, device_id_type=MESH
         )
+
+    list_copy = pltpu.make_async_copy(lists_in, lists, list_sem.at[0])
+    count_copy = pltpu.make_async_copy(counts_in, counts, list_sem.at[1])
+    list_copy.start()
+    count_copy.start()
 
     barrier = pltpu.get_barrier_semaphore()
 
@@ -89,25 +96,9 @@
     def _():
         hello(at(z + 1, x, y, 0))
 
-    @pl.when(both(quarter == 0, not_first))
-    def _():
-        for i in range(8):
-            hello(at(z - 1, (i // 4) * 2 + 1, i % 4, 1))
-
-    @pl.when(both(quarter == 3, not_last))
-    def _():
-        for i in range(4):
-            hello(at(z + 1, 0, i, 0))
-
-    halo_up = both(b == 3, not_last)
-    halo_down = both(both(b == 0, u < 4), not_first)
     pl.semaphore_wait(
         barrier,
-        31
-        + jnp.where(both(c == 1, not_last), 1, 0)
-        + jnp.where(both(c == 0, not_first), 1, 0)
-        + jnp.where(halo_up, 8, 0)
-        + jnp.where(halo_down, 8, 0),
+        31 + jnp.where(both(c == 1, not_last), 1, 0) + jnp.where(both(c == 0, not_first), 1, 0),
     )
 
     e = b % 2
@@ -139,7 +130,7 @@
             dst = target.at[rows(row, size), :]
 
             def away():
-                remote(src, dst, send.at[s], sem, at(z, px, pp * 2 + xl, e)).start()
+                remote(src, dst, send.at[s], sem, at(z, px, pp * 2 + (xl + z) % 2, e)).start()
 
             if (dx, dp) != (0, 0):
                 away()
@@ -152,29 +143,26 @@
                 def _():
                     away()
 
-    sends_prev = either(b == 1, halo_up)
-    sends_next = either(both(b == 2, u < 4), halo_down)
+    sends_prev, sends_next = b == 1, both(b == 2, u < 4)
 
     def scatter_halo(source, target, a):
         @pl.when(sends_prev)
         def _():
-            up_z, odd = jnp.where(b == 3, 1, 0), jnp.where(b == 1, 1, 0)
             for dx, dp in PAIR_OFFSETS:
                 px, pp = (x + dx) % 4, (y // 2 + dp) % 2
                 remote(
                     source.at[:, columns(MAIN + px * 2 + pp)], target.at[rows(u * KROWS, KROWS), :],
-                    halo_send.at[a], halo_got.at[a], at(z + up_z, px, pp * 2 + odd, 0),
+                    halo_send.at[a], halo_got.at[a], at(z, px, pp * 2 + (1 + z) % 2, 0),
                 ).start()
 
         @pl.when(sends_next)
         def _():
-            down_z = jnp.where(b == 0, 1, 0)
             for dx, dp in PAIR_OFFSETS:
                 px, pp = (x + dx) % 4, (y // 2 + dp) % 2
                 remote(
                     source.at[:, columns(MAIN + px * 2 + pp)],
                     target.at[rows(2 * BLOCK + (u % 4) * KROWS, KROWS), :],
-                    halo_send.at[a], halo_got.at[a], at(z - down_z, px, pp * 2 + down_z, 1),
+                    halo_send.at[a], halo_got.at[a], at(z, px, pp * 2 + z % 2, 1),
                 ).start()
 
     kv_row, q_row = BLOCK * (1 + e) + u * KROWS, HALF * e + u * QROWS
@@ -200,32 +188,24 @@
             ),
         )
 
-    from_prev, from_next = either(c == 1, not_first), either(c == 0, not_last)
-
     def pass_on(i, target):
         to_up, to_down = halos(i, target)
         arrived(target.at[pl.ds(2 * BLOCK, BLOCK), :], got.at[2 * i + 1])
-
-        @pl.when(up)
-        def _():
-            to_up.start()
-
         arrived(target.at[pl.ds(BLOCK, BLOCK), :], got.at[2 * i])
-
-        @pl.when(down)
-        def _():
-            to_down.start()
-
-    def halos_in(i, target):
+        pl.when(c == 0)(to_up.start)
+        pl.when(c == 1)(to_down.start)
+        pl.when(both(c == 1, not_last))(to_up.start)
+        pl.when(both(c == 0, not_first))(to_down.start)
+
+    def near_in(i, target):
         to_up, to_down = halos(i, target)
-
-        @pl.when(from_prev)
-        def _():
-            to_up.wait_recv()
-
-        @pl.when(from_next)
-        def _():
-            to_down.wait_recv()
+        pl.when(c == 1)(to_up.wait_recv)
+        pl.when(c == 0)(to_down.wait_recv)
+
+    def far_in(i, target):
+        to_up, to_down = halos(i, target)
+        pl.when(both(c == 0, not_first))(to_up.wait_recv)
+        pl.when(both(c == 1, not_last))(to_down.wait_recv)
 
     def halos_sent(i, target):
         to_up, to_down = halos(i, target)
@@ -238,59 +218,58 @@
         def _():
             to_down.wait_send()
 
-    def shared_halo(a, target):
+    def shared_copies(a, target):
+        block, half = target.at[pl.ds(BLOCK, BLOCK), :], target.at[pl.ds(BLOCK, HALF), :]
+        prev, after = target.at[pl.ds(0, BLOCK), :], target.at[pl.ds(2 * BLOCK, HALF), :]
+        near, far = (fwd_send.at[8 + a], fwd_got.at[8 + a]), (fwd_send.at[10 + a], fwd_got.at[10 + a])
         return (
-            remote(
-                target.at[pl.ds(BLOCK, BLOCK), :], target.at[pl.ds(0, BLOCK), :],
-                fwd_send.at[8 + a], fwd_got.at[8 + a], at(z, x, y, 1),
-            ),
-            remote(
-                target.at[pl.ds(BLOCK, HALF), :], target.at[pl.ds(2 * BLOCK, HALF), :],
-                fwd_send.at[8 + a], fwd_got.at[8 + a], at(z, x, y, 0),
-            ),
+            (c == 0, c == 1, remote(block, prev, *near, at(z, x, y, 1))),
+            (c == 1, c == 0, remote(half, after, *near, at(z, x, y, 0))),
+            (both(quarter == 3, not_last), both(quarter == 0, not_first), remote(block, prev, *far, at(z + 1, x, y, 0))),
+            (both(quarter == 0, not_first), both(quarter == 3, not_last), remote(half, after, *far, at(z - 1, x, y, 1))),
         )
 
-    def shared_pass_on(a, target):
-        to_other, to_first = shared_halo(a, target)
+    def own_shared(a, target):
         arrived(target.at[pl.ds(BLOCK, BLOCK), :], got.at[8 + a])
 
-        @pl.when(c == 0)
-        def _():
-            to_other.start()
-
-        @pl.when(c == 1)
-        def _():
-            to_first.start()
+    def relay(a, target):
+        @pl.when(outer)
+        def _():
+            own_shared(a, target)
+            for sends, _, copy in shared_copies(a, target)[2:]:
+                pl.when(sends)(copy.start)
+
+    def share(a, target):
+        @pl.when(no(outer))
+        def _():
+            own_shared(a, target)
+
+        for sends, _, copy in shared_copies(a, target)[:2]:
+            pl.when(sends)(copy.start)
 
     def shared_in(a, target):
-        to_other, to_first = shared_halo(a, target)
-
-        @pl.when(both(c == 0, either(quarter == 2, not_first)))
+        @pl.when(quarter == 2)
         def _():
             arrived(target.at[pl.ds(0, BLOCK), :], halo_got.at[a])
 
-        @pl.when(both(c == 1, either(quarter == 1, not_last)))
+        @pl.when(quarter == 1)
         def _():
             arrived(target.at[pl.ds(2 * BLOCK, HALF), :], halo_got.at[a])
 
-        @pl.when(c == 0)
-        def _():
-            to_other.wait_send()
-            to_first.wait_recv()
-
-        @pl.when(c == 1)
-        def _():
-            to_first.wait_send()
-            to_other.wait_recv()
-
-    def lay_out(keys, values, tiles):
+        for sends, gets, copy in shared_copies(a, target):
+            pl.when(sends)(copy.wait_send)
+            pl.when(gets)(copy.wait_recv)
+
+    def lay_out(keys, values, start, stop):
         def one(t, carry):
             row = pl.ds(pl.multiple_of(t * TILE, TILE), TILE)
-            kt[t] = keys[row, :]
-            vt[t, 0:HD, :] = values[row, :].T
+            if keys is not None:
+                kt[t] = keys[row, :]
+            if values is not None:
+                vt[t, 0:HD, :] = values[row, :].T
             return carry
 
-        lax.fori_loop(0, tiles, one, 0)
+        lax.fori_loop(start, stop, one, 0)
 
     def attend(queries, query_row, block, first_block, done_row, tiles):
         def scale(t, carry):
@@ -301,7 +280,6 @@
             qt[t, HD:2 * HD, :] = (query - high.astype(jnp.float32)).astype(jnp.bfloat16)
             return carry
 
-        lax.fori_loop(0, FT, scale, 0)
         first = first_block * 6
 
         def place(tile, m):
@@ -328,6 +306,11 @@
                 part = jnp.dot(vt[place(tile, m)], w, preferred_element_type=jnp.float32)
                 total = part if total is None else total + part
             return total
+
+        def put(t):
+            total = acc[...]
+            row = pl.multiple_of(done_row + t * TILE, TILE)
+            done[pl.ds(row, TILE), :] = (total[:HD] / total[HD:HD + 1]).T.astype(jnp.bfloat16)
 
         def query_tile(t, peak):
             acc[...] = jnp.zeros_like(acc)
@@ -346,12 +329,42 @@
                 return highest
 
             peak = lax.fori_loop(0, GROUPS // 2, step, peak)
-            total = acc[...]
-            row = pl.multiple_of(done_row + t * TILE, TILE)
-            done[pl.ds(row, TILE), :] = (total[:HD] / total[HD:HD + 1]).T.astype(jnp.bfloat16)
+            put(t)
             return peak
 
-        lax.fori_loop(0, FT, query_tile, scores(s0, 0, 0))
+        def all_tiles():
+            lax.fori_loop(0, FT, scale, 0)
+            lax.fori_loop(0, FT, query_tile, scores(s0, 0, 0))
+
+        def keep(t, carry):
+            def step(g, peak):
+                return jnp.maximum(peak, scores(kept.at[t * GROUPS + g], t, g))
+
+            peaks[t] = lax.fori_loop(0, GROUPS, step, jnp.full((1, TILE), -FAR, jnp.float32))
+            return carry
+
+        def finish(t, carry):
+            peak = peaks[t]
+            acc[...] = jnp.zeros_like(acc)
+
+            def step(i, carry):
+                g = 2 * i
+                part = weigh(kept.at[t * GROUPS + g], t, g, peak)
+                acc[...] += part + weigh(kept.at[t * GROUPS + g + 1], t, g + 1, peak)
+                return carry
+
+            lax.fori_loop(0, GROUPS // 2, step, 0)
+            put(t)
+            return carry
+
+        def first_stage():
+            lax.fori_loop(0, FT, scale, 0)
+            lax.fori_loop(0, FT, keep, 0)
+
+        def second_stage():
+            lax.fori_loop(0, FT, finish, 0)
+
+        return all_tiles, first_stage, second_stage
 
     def give_back(done_row, head, half, core, local, s):
         for dh, dy in HALF_OFFSETS:
@@ -374,45 +387,74 @@
                     away()
 
     def unit(queries, r, e):
-        attend(queries, e * HALF, 4 * z + 2 * c + e, 4 * z + 2 * c - 1, (2 * r + e) * HALF, PAIR // TILE)
+        return attend(
+            queries, e * HALF, 4 * z + 2 * c + e, 4 * z + 2 * c - 1, (2 * r + e) * HALF, PAIR // TILE
+        )
+
+    def return_unit(r, e):
         give_back((2 * r + e) * HALF, chip * 2 + r, c, e, both(mine, c == e), r)
 
+    inner_e, outer_e = 1 - c, c
+    near_tiles = (jnp.where(c == 0, 6, 0), jnp.where(c == 0, 21, 18))
+    far_tiles = (jnp.where(c == 0, 0, 18), jnp.where(c == 0, 6, 21))
+    send_q(0, qa)
     send_k(0, ka)
     send_v(0, va)
-    send_q(0, qa)
     vt[:, HD:VROWS, :] = jnp.ones((vt.shape[0], VROWS - HD, TILE), jnp.bfloat16)
+    list_copy.wait()
+    count_copy.wait()
     pass_on(0, ka)
+    send_q(1, qb)
+    pass_on(1, va)
     send_k(1, kb)
-    pass_on(1, va)
     send_v(1, vb)
-    send_q(1, qb)
     arrived(qa, q_got.at[0])
-    halos_in(0, ka)
-    halos_in(1, va)
-    lay_out(ka, va, PAIR // TILE)
-    unit(qa, 0, 0)
+    near_in(0, ka)
+    near_in(1, va)
+    lay_out(ka, va, *near_tiles)
+    unit(qa, 0, inner_e)[0]()
     pass_on(2, kb)
+    scatter_shared(q, ql, u * QROWS, QROWS, 8, q_got.at[2])
     scatter_shared(k, kl, BLOCK + u * KROWS, KROWS, 6, got.at[8])
     scatter_halo(k, kl, 0)
-    unit(qa, 0, 1)
+    far_in(0, ka)
+    far_in(1, va)
+    lay_out(ka, va, *far_tiles)
+    unit(qa, 0, outer_e)[0]()
     pass_on(3, vb)
     scatter_shared(v, vl, BLOCK + u * KROWS, KROWS, 7, got.at[9])
     scatter_halo(v, vl, 1)
-    scatter_shared(q, ql, u * QROWS, QROWS, 8, q_got.at[2])
     arrived(qb, q_got.at[1])
-    halos_in(2, kb)
-    halos_in(3, vb)
-    lay_out(kb, vb, PAIR // TILE)
-    unit(qb, 1, 0)
-    shared_pass_on(0, kl)
-    unit(qb, 1, 1)
-    shared_pass_on(1, vl)
+    near_in(2, kb)
+    lay_out(kb, None, *near_tiles)
+    _, first_stage, second_stage = unit(qb, 1, inner_e)
+    first_stage()
+    near_in(3, vb)
+    lay_out(None, vb, *near_tiles)
+    second_stage()
+    relay(0, kl)
+    share(0, kl)
+    return_unit(0, inner_e)
+    return_unit(0, outer_e)
+    return_unit(1, inner_e)
+    far_in(2, kb)
+    far_in(3, vb)
+    lay_out(kb, vb, *far_tiles)
+    unit(qb, 1, outer_e)[0]()
+    relay(1, vl)
+    share(1, vl)
+    return_unit(1, outer_e)
     arrived(ql, q_got.at[2])
     shared_in(0, kl)
+    lay_out(kl, None, 0, ONE // TILE)
+    _, first_stage, second_stage = attend(
+        ql, 0, 4 * z + quarter, 4 * z + quarter - 1, 4 * HALF, ONE // TILE
+    )
+    first_stage()
     shared_in(1, vl)
-    lay_out(kl, vl, ONE // TILE)
-    attend(ql, 0, 4 * z + quarter, 4 * z + quarter - 1, 4 * HALF, ONE // TILE)
-    give_back(4 * HALF, MAIN + chip // 2, y % 2, c, mine_l, 2)
+    lay_out(None, vl, 0, ONE // TILE)
+    second_stage()
+    give_back(4 * HALF, MAIN + chip // 2, side, c, mine_l, 2)
 
     for i, target in enumerate((ka, va, kb, vb)):
         halos_sent(i, target)
@@ -445,7 +487,7 @@
 
 def per_device(queries, keys, values, tile_lists, tile_counts):
     anywhere = pl.BlockSpec(memory_space=pl.ANY)
-    scalars = pl.BlockSpec(memory_space=pltpu.SMEM)
+    far = pl.BlockSpec(memory_space=pltpu.HBM)
     dma = pltpu.SemaphoreType.DMA
 
     def held(n):
@@ -454,9 +496,10 @@
     return pl.pallas_call(
         kernel,
         out_shape=jax.ShapeDtypeStruct((QROWS, HEADS * HD), jnp.bfloat16),
-        in_specs=[scalars, scalars, anywhere, anywhere, anywhere],
+        in_specs=[far] * 5,
         out_specs=anywhere,
         scratch_shapes=[
+            pltpu.SMEM(tile_lists.shape, jnp.int32), pltpu.SMEM(tile_counts.shape, jnp.int32), dma((2,)),
             held(2 * HALF), held(2 * HALF), held(HALF),
             held(PAIR), held(PAIR), held(ONE),
             held(PAIR), held(PAIR), held(ONE),
@@ -467,10 +510,12 @@
             pltpu.VMEM((G * TILE, TILE), jnp.float32),
             pltpu.VMEM((G * TILE, TILE), jnp.float32),
             pltpu.VMEM((VROWS, TILE), jnp.float32),
-            dma((9,)), dma((10,)), dma((3,)), dma((10,)), dma((10,)), dma((2,)), dma((2,)), dma((3,)), dma,
+            pltpu.VMEM((FT * GROUPS, G * TILE, TILE), jnp.float32),
+            pltpu.VMEM((FT, 1, TILE), jnp.float32),
+            dma((9,)), dma((10,)), dma((3,)), dma((12,)), dma((12,)), dma((2,)), dma((2,)), dma((3,)), dma,
         ],
         compiler_params=pltpu.CompilerParams(
-            collective_id=0, has_side_effects=True, vmem_limit_bytes=60 * 1024 * 1024
+            collective_id=0, has_side_effects=True, vmem_limit_bytes=54 * 1024 * 1024
         ),
         name="attention",
     )(tile_lists, tile_counts, queries, keys, values)

time: 138 us -> 128 us (0.928)
  the two profiles are of different devices: /device:TPU:66 before, /device:TPU:64 now
where the time goes in v3:
time: 128 us; the launch traced here: 126 us
  Pallas kernels  122 us (95%)
  local copies, waits for them, and re-layouts  3.96 us (3%)
    pallas_call x1, Pallas kernels, per_device(): pl.pallas_call(kernel, out_shape=jax.ShapeDtypeStruct((QROWS, HEADS * HD)...  122 us
    unnamed x2, local copies, waits for them, and re-layouts  3.96 us

profile of v3, /device:TPU:64, one launch (start us, length us, event | category | flops | bytes accessed | tf_op | source)
XLA Modules:
  0.0 125.6 jit_solution(2073347988315618889)
XLA Ops:
  0.0 1.4 %copy.6.lists_in = s32[48,12]{1,0:T(8,128)} copy(s32[48,12]{0,1:T(8,128)} %param.8) | data formatting | bytes 4608 | tf_op args[3]
  1.4 121.6 %attention.1 = bf16[144,5120]{1,0:T(8,128)(2,1)} custom-call(s32[48,12]{1,0:T(8,128)} %copy.6.lists_in, s32[48]{0:T(128)} %counts_in.1, bf16[144,5120]{1,0:T(8,128)(2,1)} %q.1, bf16[288,5120]{1,0:T(8,128)(2,1)} %k.1, bf16[288,5120]{1,0:T(8,128)(2,1)} %v.1), custom_call_target="tpu_custom_call" | custom-call | tf_op jit(solution)/shard_map/attention/pallas_call | solution.py:496
  123.0 2.6 %copy.8 = bf16[144,5120]{1,0:T(8,128)(2,1)} copy(bf16[144,5120]{1,0:T(8,128)(2,1)} %attention.1) | data formatting | bytes 2949120

commit v4 on v3

--- a/solution.py
+++ b/solution.py
@@ -20,7 +20,7 @@
 PAIR = 3 * BLOCK + HALF
 ONE = 2 * BLOCK + HALF
 VROWS = HD + 16
-G = 3
+G = 6
 GROUPS = MAXT // G
 LOG2_SCALE = HD ** (-0.5) * 1.4426950408889634
 FAR = 1e30
@@ -283,7 +283,7 @@
         first = first_block * 6
 
         def place(tile, m):
-            return jnp.clip(lists[tile, m] - first, 0, tiles - 1)
+            return jnp.clip(lists[m, tile] - first, 0, tiles - 1)
 
         def scores(buffer, t, g):
             tile = block * FT + t
@@ -408,15 +408,15 @@
     pass_on(1, va)
     send_k(1, kb)
     send_v(1, vb)
+    scatter_shared(q, ql, u * QROWS, QROWS, 8, q_got.at[2])
+    scatter_shared(k, kl, BLOCK + u * KROWS, KROWS, 6, got.at[8])
+    scatter_halo(k, kl, 0)
     arrived(qa, q_got.at[0])
     near_in(0, ka)
     near_in(1, va)
     lay_out(ka, va, *near_tiles)
     unit(qa, 0, inner_e)[0]()
     pass_on(2, kb)
-    scatter_shared(q, ql, u * QROWS, QROWS, 8, q_got.at[2])
-    scatter_shared(k, kl, BLOCK + u * KROWS, KROWS, 6, got.at[8])
-    scatter_halo(k, kl, 0)
     far_in(0, ka)
     far_in(1, va)
     lay_out(ka, va, *far_tiles)
@@ -499,7 +499,7 @@
         in_specs=[far] * 5,
         out_specs=anywhere,
         scratch_shapes=[
-            pltpu.SMEM(tile_lists.shape, jnp.int32), pltpu.SMEM(tile_counts.shape, jnp.int32), dma((2,)),
+            pltpu.SMEM(tile_lists.shape[::-1], jnp.int32), pltpu.SMEM(tile_counts.shape, jnp.int32), dma((2,)),
             held(2 * HALF), held(2 * HALF), held(HALF),
             held(PAIR), held(PAIR), held(ONE),
             held(PAIR), held(PAIR), held(ONE),
@@ -515,10 +515,10 @@
             dma((9,)), dma((10,)), dma((3,)), dma((12,)), dma((12,)), dma((2,)), dma((2,)), dma((3,)), dma,
         ],
         compiler_params=pltpu.CompilerParams(
-            collective_id=0, has_side_effects=True, vmem_limit_bytes=54 * 1024 * 1024
+            collective_id=0, has_side_effects=True, vmem_limit_bytes=52 * 1024 * 1024
         ),
         name="attention",
-    )(tile_lists, tile_counts, queries, keys, values)
+    )(tile_lists.T, tile_counts, queries, keys, values)
 
 
 def solution(mesh):

time: 128 us -> 125 us (0.977); the launches traced: 126 us -> 124 us
  local copies, waits for them, and re-layouts: 3.96 us -> 2.46 us
    unnamed x2 -> x5, local copies, waits for them, and re-layouts: 3.96 us -> 2.46 us
where the time goes in v4:
time: 125 us; the launch traced here: 124 us
  Pallas kernels  121 us (97%)
  local copies, waits for them, and re-layouts  2.46 us (2%)
    pallas_call x1, Pallas kernels, per_device(): pl.pallas_call(kernel, out_shape=jax.ShapeDtypeStruct((QROWS, HEADS * HD)...  121 us

profile of v4, /device:TPU:64, one launch (start us, length us, event | category | flops | bytes accessed | tf_op | source)
XLA Modules:
  0.0 123.9 jit_solution(12956214970380352651)
XLA Ops:
  0.0 0.0 copy-start
  0.0 0.7 copy-done
  0.7 0.0 copy-start.1
  0.7 0.7 copy-done.1
  1.4 121.4 %attention.1 = bf16[144,5120]{1,0:T(8,128)(2,1)S(1)} custom-call(s32[12,48]{1,0:T(8,128)S(1)} %bitcast.1, s32[48]{0:T(128)S(1)} %copy-done.1, bf16[144,5120]{1,0:T(8,128)(2,1)} %q.1, bf16[288,5120]{1,0:T(8,128)(2,1)} %k.1, bf16[288,5120]{1,0:T(8,128)(2,1)} %v.1), custom_call_target="tpu_custom_call" | custom-call | tf_op jit(solution)/shard_map/attention/pallas_call | solution.py:496
  122.8 1.1 copy.7
Async XLA Ops:
  0.0 0.7 copy-start
  0.7 0.7 copy-start.1

commit v5 on v4

--- a/solution.py
+++ b/solution.py
@@ -434,8 +434,6 @@
     second_stage()
     relay(0, kl)
     share(0, kl)
-    return_unit(0, inner_e)
-    return_unit(0, outer_e)
     return_unit(1, inner_e)
     far_in(2, kb)
     far_in(3, vb)
@@ -443,6 +441,8 @@
     unit(qb, 1, outer_e)[0]()
     relay(1, vl)
     share(1, vl)
+    return_unit(0, inner_e)
+    return_unit(0, outer_e)
     return_unit(1, outer_e)
     arrived(ql, q_got.at[2])
     shared_in(0, kl)

time: 125 us -> 123 us (0.984)
    pallas_call x1, Pallas kernels: 121 us -> 120 us  [per_device(): pl.pallas_call(kernel, out_shape=jax.ShapeDtypeStruct((QROWS, HEADS * HD)...]
where the time goes in v5:
time: 123 us; the launch traced here: 122 us
  Pallas kernels  120 us (98%)
  local copies, waits for them, and re-layouts  2.46 us (2%)
    pallas_call x1, Pallas kernels, per_device(): pl.pallas_call(kernel, out_shape=jax.ShapeDtypeStruct((QROWS, HEADS * HD)...  120 us
    unnamed x5, local copies, waits for them, and re-layouts  2.46 us

profile of v5, /device:TPU:64, one launch (start us, length us, event | category | flops | bytes accessed | tf_op | source)
XLA Modules:
  0.0 122.4 jit_solution(221545314842305790)
XLA Ops:
  0.0 0.0 copy-start
  0.0 0.7 copy-done
  0.7 0.0 copy-start.1
  0.7 0.7 copy-done.1
  1.4 119.9 %attention.1 = bf16[144,5120]{1,0:T(8,128)(2,1)S(1)} custom-call(s32[12,48]{1,0:T(8,128)S(1)} %bitcast.1, s32[48]{0:T(128)S(1)} %copy-done.1, bf16[144,5120]{1,0:T(8,128)(2,1)} %q.1, bf16[288,5120]{1,0:T(8,128)(2,1)} %k.1, bf16[288,5120]{1,0:T(8,128)(2,1)} %v.1), custom_call_target="tpu_custom_call" | custom-call | tf_op jit(solution)/shard_map/attention/pallas_call | solution.py:496
  121.2 1.1 copy.7
Async XLA Ops:
  0.0 0.7 copy-start
  0.7 0.7 copy-start.1

commit v6 on v5

--- a/solution.py
+++ b/solution.py
@@ -20,7 +20,7 @@
 PAIR = 3 * BLOCK + HALF
 ONE = 2 * BLOCK + HALF
 VROWS = HD + 16
-G = 6
+G = 3
 GROUPS = MAXT // G
 LOG2_SCALE = HD ** (-0.5) * 1.4426950408889634
 FAR = 1e30

time: 123 us -> 124 us (level)
  Pallas kernels: 120 us -> 122 us
    pallas_call x1, Pallas kernels: 120 us -> 122 us  [per_device(): pl.pallas_call(kernel, out_shape=jax.ShapeDtypeStruct((QROWS, HEADS * HD)...]
where the time goes in v6:
time: 124 us
  Pallas kernels  122 us (98%)
  local copies, waits for them, and re-layouts  2.46 us (2%)
    pallas_call x1, Pallas kernels, per_device(): pl.pallas_call(kernel, out_shape=jax.ShapeDtypeStruct((QROWS, HEADS * HD)...  122 us

profile of v6, /device:TPU:64, one launch (start us, length us, event | category | flops | bytes accessed | tf_op | source)
XLA Modules:
  0.0 124.1 jit_solution(14583763809268422264)
XLA Ops:
  0.0 0.0 copy-start
  0.0 0.7 copy-done
  0.7 0.0 copy-start.1
  0.7 0.7 copy-done.1
  1.4 121.6 %attention.1 = bf16[144,5120]{1,0:T(8,128)(2,1)S(1)} custom-call(s32[12,48]{1,0:T(8,128)S(1)} %bitcast.1, s32[48]{0:T(128)S(1)} %copy-done.1, bf16[144,5120]{1,0:T(8,128)(2,1)} %q.1, bf16[288,5120]{1,0:T(8,128)(2,1)} %k.1, bf16[288,5120]{1,0:T(8,128)(2,1)} %v.1), custom_call_target="tpu_custom_call" | custom-call | tf_op jit(solution)/shard_map/attention/pallas_call | solution.py:496
  123.0 1.1 copy.7
Async XLA Ops:
  0.0 0.7 copy-start
  0.7 0.7 copy-start.1

commit v7 on v5

--- a/solution.py
+++ b/solution.py
@@ -434,7 +434,6 @@
     second_stage()
     relay(0, kl)
     share(0, kl)
-    return_unit(1, inner_e)
     far_in(2, kb)
     far_in(3, vb)
     lay_out(kb, vb, *far_tiles)
@@ -443,6 +442,7 @@
     share(1, vl)
     return_unit(0, inner_e)
     return_unit(0, outer_e)
+    return_unit(1, inner_e)
     return_unit(1, outer_e)
     arrived(ql, q_got.at[2])
     shared_in(0, kl)

time: 123 us -> 122 us (level)
  no operation moved by 1% of the time
where the time goes in v7:
time: 122 us; the launch traced here: 121 us
  Pallas kernels  119 us (98%)
  local copies, waits for them, and re-layouts  2.46 us (2%)
    pallas_call x1, Pallas kernels, per_device(): pl.pallas_call(kernel, out_shape=jax.ShapeDtypeStruct((QROWS, HEADS * HD)...  119 us
    unnamed x5, local copies, waits for them, and re-layouts  2.46 us

profile of v7, /device:TPU:64, one launch (start us, length us, event | category | flops | bytes accessed | tf_op | source)
XLA Modules:
  0.0 121.4 jit_solution(3328277578829761750)
XLA Ops:
  0.0 0.0 copy-start
  0.0 0.7 copy-done
  0.7 0.0 copy-start.1
  0.7 0.7 copy-done.1
  1.4 119.0 %attention.1 = bf16[144,5120]{1,0:T(8,128)(2,1)S(1)} custom-call(s32[12,48]{1,0:T(8,128)S(1)} %bitcast.1, s32[48]{0:T(128)S(1)} %copy-done.1, bf16[144,5120]{1,0:T(8,128)(2,1)} %q.1, bf16[288,5120]{1,0:T(8,128)(2,1)} %k.1, bf16[288,5120]{1,0:T(8,128)(2,1)} %v.1), custom_call_target="tpu_custom_call" | custom-call | tf_op jit(solution)/shard_map/attention/pallas_call | solution.py:496
  120.3 1.1 copy.7
Async XLA Ops:
  0.0 0.7 copy-start
  0.7 0.7 copy-start.1
